TPU v7x, 256 devices: a whole 4x4x8 slice. The times are simulated.
256 devices in a mesh: wide: 16 (over z, x_lo), narrow: 16 (over x_hi, y, core).
Axes of the slice: x: 4 (x_hi: 2, x_lo: 2; x = x_hi * 2 + x_lo), y: 4, z: 8, core: 2. Of those that a mesh axis runs over, the one named last changes fastest.
Arguments:
- panel: float32 [16, 2097152], P(None, ('wide', 'narrow'))
- signs: int32 [2097152], P(('wide', 'narrow')), may hold values from -1 to 1, as said below
- samples: int32 [16384], replicated, may hold values from 0 to 2097151, as said below
Outputs:
- mixed: float32 [16, 2097152], P(None, ('wide', 'narrow'))
- gram: float32 [16, 16], replicated
Inputs may be any that keep to these rules, and one draw needn't show every extreme that they name: `signs`: every entry is -1 or 1. `samples`: indices may repeat; the first is 0 and the last is 2097151.
All inputs are finite; a program needn't handle non-finite values.
Results may differ from a plain program's by a relative error of at most 0.000098.
Values sent between devices are 32-bit elements; how exact they have to be, the bound alone decides.
No kernel may reach another device: no remote copies, remote signals or barrier semaphores. Data moves between devices by JAX's collectives and lax.ppermute only.
A program may use at most 64 MiB of HBM per device.

v0:
```python
import jax
import jax.numpy as jnp
from jax import lax
from jax.sharding import PartitionSpec as P


def partner_2(value, axis, stride):
    mask = 2**stride
    pairs = [(source, source ^ mask) for source in range(lax.axis_size(axis))]
    return lax.ppermute(value, axis, pairs)


def hadamard(order):
    bits = order.bit_length() - 1
    first = jnp.arange(order, dtype=jnp.int32)[:, None]
    second = jnp.arange(order, dtype=jnp.int32)[None, :]
    parity = jnp.zeros((order, order), jnp.int32)
    for level in range(bits):
        parity = parity + (first >> level & 1) * (second >> level & 1)
    return jnp.where(parity % 2 == 0, 1.0, -1.0).astype(jnp.float32)


def per_device(panel, signs, samples):
    high = lax.Precision.HIGHEST
    columns, local_rows = panel.shape
    blocks = local_rows // 128
    flipped = panel * signs.astype(jnp.float32)[None, :]
    shaped = flipped.reshape(columns, blocks, 128)
    shaped = jnp.einsum("pbc,ec->pbe", shaped, hadamard(128), precision=high)
    shaped = jnp.einsum("pbc,eb->pec", shaped, hadamard(blocks), precision=high)
    current = shaped.reshape(columns, local_rows)
    narrow_count = lax.axis_size("narrow")
    wide_count = lax.axis_size("wide")
    narrow_place = lax.axis_index("narrow")
    for level in range(narrow_count.bit_length() - 1):
        partner = partner_2(current, "narrow", level)
        current = jnp.where(narrow_place >> level & 1 == 0, current + partner, partner - current)
    wide_place = lax.axis_index("wide")
    for level in range(wide_count.bit_length() - 1):
        partner = partner_2(current, "wide", level)
        current = jnp.where(wide_place >> level & 1 == 0, current + partner, partner - current)
    total_rows = local_rows * narrow_count * wide_count
    mixed = current * (1.0 / jnp.sqrt(jnp.float32(total_rows)))
    device_place = lax.axis_index("wide") * narrow_count + lax.axis_index("narrow")
    offsets = samples - device_place * local_rows
    inside = jnp.logical_and(offsets >= 0, offsets < local_rows)
    clipped = jnp.clip(offsets, 0, local_rows - 1)
    picked = jnp.take(mixed, clipped, axis=1) * inside.astype(jnp.float32)[None, :]
    partial_gram = jnp.dot(picked, picked.T, precision=high, preferred_element_type=jnp.float32)
    total_gram = lax.psum(partial_gram, ("wide", "narrow"))
    gram = total_gram / jnp.float32(samples.shape[0])
    return (mixed, gram)


def solution(mesh):
    placed = (P(None, ("wide", "narrow")), P(("wide", "narrow")), P())
    return jax.shard_map(
        per_device,
        mesh=mesh,
        in_specs=placed,
        out_specs=(P(None, ("wide", "narrow")), P()),
        check_vma=False,
    )
```

profile of v0, /device:TPU:1, one launch (start us, length us, event | category | flops | bytes accessed | tf_op | source)
XLA Modules:
  0.0 373.8 jit_solution(9968325390276020278)
XLA Ops:
  0.7 0.8 convert_element_type.6
  1.5 1.1 multiply_bitcast_fusion
  2.7 0.7 fusion.8
  3.4 0.6 fusion.18
  4.1 0.3 copy.38
  4.4 3.3 collective-permute-start
  7.7 2.6 copy.9
  10.3 2.6 copy.10
  13.0 5.9 %subtract_select_fusion.6 = f32[16,8192]{0,1:T(8,128)} fusion(f32[16,8192]{0,1:T(8,128)} %copy.10, f32[16,8192]{0,1:T(8,128)} %copy.9, pred[]{:T(512)S(6)} %eq.43), kind=kLoop, calls=%fused_computation.13 | loop fusion | flops 393216 | bytes 1572865 | tf_op jit(solution)/shard_map/jit(_where)/select_n | solution.py:37
  18.8 2.8 copy.13
  21.7 13.5 %collective-permute-done.1 = f32[16,8192]{1,0:T(8,128)S(1)} collective-permute-done((f32[16,8192]{1,0:T(8,128)S(1)}, f32[16,8192]{1,0:T(8,128)S(1)}, u32[]{:S(2)}, u32[]{:S(2)}) %collective-permute-start.1) | collective-permute-done | bytes 524320 | tf_op jit(solution)/shard_map/ppermute | solution.py:10
  35.3 2.6 copy.14
  37.9 5.8 %subtract_select_fusion.5 = f32[16,8192]{0,1:T(8,128)} fusion(f32[16,8192]{0,1:T(8,128)} %copy.14, f32[16,8192]{0,1:T(8,128)} %subtract_select_fusion.6, pred[]{:T(512)S(6)} %eq.42), kind=kLoop, calls=%fused_computation.12 | loop fusion | flops 393216 | bytes 1572865 | tf_op jit(solution)/shard_map/jit(_where)/select_n | solution.py:37
  43.7 2.8 copy.16
  46.5 1.3 collective-permute-start.2
  47.8 13.0 %collective-permute-done.2 = f32[16,8192]{1,0:T(8,128)S(1)} collective-permute-done((f32[16,8192]{1,0:T(8,128)S(1)}, f32[16,8192]{1,0:T(8,128)S(1)}, u32[]{:S(2)}, u32[]{:S(2)}) %collective-permute-start.2) | collective-permute-done | bytes 524320 | tf_op jit(solution)/shard_map/ppermute | solution.py:10
  60.7 2.6 copy.17
  63.4 5.9 %subtract_select_fusion.4 = f32[16,8192]{0,1:T(8,128)} fusion(f32[16,8192]{0,1:T(8,128)} %copy.17, f32[16,8192]{0,1:T(8,128)} %subtract_select_fusion.5, pred[]{:T(512)S(6)} %eq.41), kind=kLoop, calls=%fused_computation.11 | loop fusion | flops 393216 | bytes 1572865 | tf_op jit(solution)/shard_map/jit(_where)/select_n | solution.py:37
  69.3 2.8 copy.19
  72.0 1.1 collective-permute-start.3
  73.1 12.2 %collective-permute-done.3 = f32[16,8192]{1,0:T(8,128)S(1)} collective-permute-done((f32[16,8192]{1,0:T(8,128)S(1)}, f32[16,8192]{1,0:T(8,128)S(1)}, u32[]{:S(2)}, u32[]{:S(2)}) %collective-permute-start.3) | collective-permute-done | bytes 524320 | tf_op jit(solution)/shard_map/ppermute | solution.py:10
  85.4 2.6 copy.20
  88.0 5.8 %subtract_select_fusion.3 = f32[16,8192]{0,1:T(8,128)} fusion(f32[16,8192]{0,1:T(8,128)} %copy.20, f32[16,8192]{0,1:T(8,128)} %subtract_select_fusion.4, pred[]{:T(512)S(6)} %eq.40), kind=kLoop, calls=%fused_computation.10 | loop fusion | flops 393216 | bytes 1572865 | tf_op jit(solution)/shard_map/jit(_where)/select_n | solution.py:37
  93.8 2.8 copy.22
  96.7 10.8 %collective-permute-done.4 = f32[16,8192]{1,0:T(8,128)S(1)} collective-permute-done((f32[16,8192]{1,0:T(8,128)S(1)}, f32[16,8192]{1,0:T(8,128)S(1)}, u32[]{:S(2)}, u32[]{:S(2)}) %collective-permute-start.4) | collective-permute-done | bytes 524320 | tf_op jit(solution)/shard_map/ppermute | solution.py:10
  107.5 2.6 copy.23
  110.1 5.9 %subtract_select_fusion.2 = f32[16,8192]{0,1:T(8,128)} fusion(f32[16,8192]{0,1:T(8,128)} %copy.23, f32[16,8192]{0,1:T(8,128)} %subtract_select_fusion.3, pred[]{:T(512)S(6)} %eq.39), kind=kLoop, calls=%fused_computation.9 | loop fusion | flops 393216 | bytes 1572865 | tf_op jit(solution)/shard_map/jit(_where)/select_n | solution.py:41
  116.0 2.8 copy.25
  118.8 0.3 collective-permute-start.5
  119.1 9.9 %collective-permute-done.5 = f32[16,8192]{1,0:T(8,128)S(1)} collective-permute-done((f32[16,8192]{1,0:T(8,128)S(1)}, f32[16,8192]{1,0:T(8,128)S(1)}, u32[]{:S(2)}, u32[]{:S(2)}) %collective-permute-start.5) | collective-permute-done | bytes 524320 | tf_op jit(solution)/shard_map/ppermute | solution.py:10
  129.0 2.6 copy.26
  131.6 5.8 %subtract_select_fusion.1 = f32[16,8192]{0,1:T(8,128)} fusion(f32[16,8192]{0,1:T(8,128)} %copy.26, f32[16,8192]{0,1:T(8,128)} %subtract_select_fusion.2, pred[]{:T(512)S(6)} %eq.38), kind=kLoop, calls=%fused_computation.8 | loop fusion | flops 393216 | bytes 1572865 | tf_op jit(solution)/shard_map/jit(_where)/select_n | solution.py:41
  137.4 2.8 copy.28
  140.2 1.7 collective-permute-start.6
  141.9 24.1 %collective-permute-done.6 = f32[16,8192]{1,0:T(8,128)S(1)} collective-permute-done((f32[16,8192]{1,0:T(8,128)S(1)}, f32[16,8192]{1,0:T(8,128)S(1)}, u32[]{:S(2)}, u32[]{:S(2)}) %collective-permute-start.6) | collective-permute-done | bytes 524320 | tf_op jit(solution)/shard_map/ppermute | solution.py:10
  166.0 2.6 copy.29
  168.7 5.9 %subtract_select_fusion = f32[16,8192]{0,1:T(8,128)} fusion(f32[16,8192]{0,1:T(8,128)} %copy.29, f32[16,8192]{0,1:T(8,128)} %subtract_select_fusion.1, pred[]{:T(512)S(6)} %eq.37), kind=kLoop, calls=%fused_computation.7 | loop fusion | flops 393216 | bytes 1572865 | tf_op jit(solution)/shard_map/jit(_where)/select_n | solution.py:41
  174.5 2.8 copy.31
  177.3 5.0 %collective-permute-start.7 = (f32[16,8192]{1,0:T(8,128)S(1)}, f32[16,8192]{1,0:T(8,128)S(1)}, u32[]{:S(2)}, u32[]{:S(2)}) collective-permute-start(f32[16,8192]{1,0:T(8,128)S(1)} %copy.31), channel_id=1, source_target_pairs={{0,128},{16,144},{32,160},{48,176},{64,192},{80,208},{96,224},{112... | collective-permute-start | bytes 1572872 | tf_op jit(solution)/shard_map/ppermute | solution.py:10
  182.4 22.9 %collective-permute-done.7 = f32[16,8192]{1,0:T(8,128)S(1)} collective-permute-done((f32[16,8192]{1,0:T(8,128)S(1)}, f32[16,8192]{1,0:T(8,128)S(1)}, u32[]{:S(2)}, u32[]{:S(2)}) %collective-permute-start.7) | collective-permute-done | bytes 524320 | tf_op jit(solution)/shard_map/ppermute | solution.py:10
  205.4 2.6 copy.32
  208.0 6.0 %select_multiply_fusion = f32[16,8192]{0,1:T(8,128)} fusion(f32[16,8192]{0,1:T(8,128)} %copy.32, f32[16,8192]{0,1:T(8,128)} %subtract_select_fusion, pred[]{:T(512)S(6)} %eq.36), kind=kLoop, calls=%fused_computation.6 | loop fusion | flops 524288 | bytes 1572865 | tf_op jit(solution)/shard_map/mul | solution.py:43
  214.0 3.5 copy.34
  217.5 56.6 %gather_fusion = f32[16384,16]{1,0:T(8,128)} fusion(f32[16,8192]{0,1:T(8,128)} %select_multiply_fusion, s32[16384]{0:T(1024)S(1)} %fusion.15), kind=kCustom, calls=%fused_computation | custom fusion | bytes 2162688 | tf_op jit(solution)/shard_map/jit(_take)/gather | solution.py:48
  274.1 6.7 %fusion.78 = f32[16384,16]{1,0:T(8,128)S(1)} fusion(f32[16384,16]{1,0:T(8,128)} %gather_fusion, f32[16384]{0:T(1024)S(1)} %get-tuple-element.7, pred[16384]{0:T(1024)(128)(4,1)S(1)} %get-tuple-element.6), kind=kLoop, calls=%fused_computation.2.clone.2 | loop fusion | flops 524288 | bytes 2179072 | tf_op jit(solution)/shard_map/dot_general | solution.py:49
  280.8 14.3 %fusion = f32[16,16]{1,0:T(8,128)S(1)} fusion(f32[16384,16]{1,0:T(8,128)S(1)} %fusion.78), kind=kOutput, calls=%fused_computation.1 | convolution fusion | flops 50331648 | bytes 1049600 | tf_op jit(solution)/shard_map/dot_general | solution.py:49
  295.1 78.1 %psum.7 = f32[16,16]{1,0:T(8,128)S(1)} all-reduce(f32[16,16]{1,0:T(8,128)S(1)} %fusion), channel_id=1, replica_groups=mesh['wide'=16,'narrow'=16] {'wide','narrow'}, use_global_device_ids=true, to_apply=%region_0.1 | all-reduce | flops 256 | bytes 2048 | tf_op jit(solution)/shard_map/psum | solution.py:50
  373.2 0.6 broadcast_multiply_fusion
  (15 shorter events, 0.4 us)
Async XLA Ops:
  4.4 5.9 %collective-permute-start = (f32[16,8192]{1,0:T(8,128)S(1)}, f32[16,8192]{1,0:T(8,128)S(1)}, u32[]{:S(2)}, u32[]{:S(2)}) collective-permute-start(f32[16,8192]{1,0:T(8,128)S(1)} %bitcast.17), channel_id=1, source_target_pairs={{0,1},{1,0},{2,3},{3,2},{4,5},{5,4},{6,7},{7,6},{8,9},{9,8},{10,11... | collective-permute-start | bytes 1572872 | tf_op jit(solution)/shard_map/ppermute | solution.py:10
  21.6 13.6 %collective-permute-start.1 = (f32[16,8192]{1,0:T(8,128)S(1)}, f32[16,8192]{1,0:T(8,128)S(1)}, u32[]{:S(2)}, u32[]{:S(2)}) collective-permute-start(f32[16,8192]{1,0:T(8,128)S(1)} %copy.13), channel_id=1, source_target_pairs={{0,2},{1,3},{2,0},{3,1},{4,6},{5,7},{6,4},{7,5},{8,10},{9,11},{10,... | collective-permute-start | bytes 1572872 | tf_op jit(solution)/shard_map/ppermute | solution.py:10
  46.5 14.2 %collective-permute-start.2 = (f32[16,8192]{1,0:T(8,128)S(1)}, f32[16,8192]{1,0:T(8,128)S(1)}, u32[]{:S(2)}, u32[]{:S(2)}) collective-permute-start(f32[16,8192]{1,0:T(8,128)S(1)} %copy.16), channel_id=1, source_target_pairs={{0,4},{1,5},{2,6},{3,7},{4,0},{5,1},{6,2},{7,3},{8,12},{9,13},{10,... | collective-permute-start | bytes 1572872 | tf_op jit(solution)/shard_map/ppermute | solution.py:10
  72.0 13.3 %collective-permute-start.3 = (f32[16,8192]{1,0:T(8,128)S(1)}, f32[16,8192]{1,0:T(8,128)S(1)}, u32[]{:S(2)}, u32[]{:S(2)}) collective-permute-start(f32[16,8192]{1,0:T(8,128)S(1)} %copy.19), channel_id=1, source_target_pairs={{0,8},{1,9},{2,10},{3,11},{4,12},{5,13},{6,14},{7,15},{8,0},{9,1},... | collective-permute-start | bytes 1572872 | tf_op jit(solution)/shard_map/ppermute | solution.py:10
  96.6 10.9 %collective-permute-start.4 = (f32[16,8192]{1,0:T(8,128)S(1)}, f32[16,8192]{1,0:T(8,128)S(1)}, u32[]{:S(2)}, u32[]{:S(2)}) collective-permute-start(f32[16,8192]{1,0:T(8,128)S(1)} %copy.22), channel_id=1, source_target_pairs={{0,16},{16,0},{32,48},{48,32},{64,80},{80,64},{96,112},{112,96},{1... | collective-permute-start | bytes 1572872 | tf_op jit(solution)/shard_map/ppermute | solution.py:10
  118.8 10.2 %collective-permute-start.5 = (f32[16,8192]{1,0:T(8,128)S(1)}, f32[16,8192]{1,0:T(8,128)S(1)}, u32[]{:S(2)}, u32[]{:S(2)}) collective-permute-start(f32[16,8192]{1,0:T(8,128)S(1)} %copy.25), channel_id=1, source_target_pairs={{0,32},{16,48},{32,0},{48,16},{64,96},{80,112},{96,64},{112,80},{1... | collective-permute-start | bytes 1572872 | tf_op jit(solution)/shard_map/ppermute | solution.py:10
  140.2 25.8 %collective-permute-start.6 = (f32[16,8192]{1,0:T(8,128)S(1)}, f32[16,8192]{1,0:T(8,128)S(1)}, u32[]{:S(2)}, u32[]{:S(2)}) collective-permute-start(f32[16,8192]{1,0:T(8,128)S(1)} %copy.28), channel_id=1, source_target_pairs={{0,64},{16,80},{32,96},{48,112},{64,0},{80,16},{96,32},{112,48},{1... | collective-permute-start | bytes 1572872 | tf_op jit(solution)/shard_map/ppermute | solution.py:10
  174.5 7.8 %copy-start = (s32[16384]{0:T(1024)S(1)}, s32[16384]{0:T(1024)}, u32[]{:S(2)}) copy-start(s32[16384]{0:T(1024)} %param.5) | copy-start | bytes 196612
  177.3 28.0 %collective-permute-start.7 = (f32[16,8192]{1,0:T(8,128)S(1)}, f32[16,8192]{1,0:T(8,128)S(1)}, u32[]{:S(2)}, u32[]{:S(2)}) collective-permute-start(f32[16,8192]{1,0:T(8,128)S(1)} %copy.31), channel_id=1, source_target_pairs={{0,128},{16,144},{32,160},{48,176},{64,192},{80,208},{96,224},{112... | collective-permute-start | bytes 1572872 | tf_op jit(solution)/shard_map/ppermute | solution.py:10
where the time goes:
time: 374 us
  waiting for transfers between devices  106 us (28%)
  local copies, waits for them, and re-layouts  104 us (28%)
  blocking collectives  78.1 us (21%)
  other arithmetic  56.2 us (15%)
  matrix products  15.7 us (4%)
  starting transfers between devices  12.8 us (3%)
    ppermute x8, waiting for transfers between devices, partner_2(): return lax.ppermute(value, axis, pairs)  106 us
    psum x1, blocking collectives, per_device(): total_gram = lax.psum(partial_gram, ('wide', 'narrow'))  78.1 us
    gather x1, local copies, waits for them, and re-layouts, per_device(): jnp.take(mixed, clipped, axis=1) * inside.astype(jnp.float32)[None, :]  56.6 us
    select_n x4, other arithmetic, per_device(): jnp.where(narrow_place >> level & 1 == 0, current + partner, partner - cu...  23.4 us
    ppermute x8, local copies, waits for them, and re-layouts, partner_2(): return lax.ppermute(value, axis, pairs)  21 us
    select_n x3, other arithmetic, per_device(): jnp.where(wide_place >> level & 1 == 0, current + partner, partner - curr...  17.6 us
    dot_general x1, matrix products, per_device(): jnp.dot(picked, picked.T, precision=high, preferred_element_type=jnp.floa...  14.3 us
    ppermute x8, starting transfers between devices, partner_2(): return lax.ppermute(value, axis, pairs)  12.8 us
  transfers between devices with their start and end apart: 8, of which 7 were waited for; matrix products, arithmetic and copies ran while one was open for 1% of the time, Pallas kernels for 0%

commit v1 on v0

--- a/solution.py
+++ b/solution.py
@@ -47,7 +47,7 @@
     clipped = jnp.clip(offsets, 0, local_rows - 1)
     picked = jnp.take(mixed, clipped, axis=1) * inside.astype(jnp.float32)[None, :]
     partial_gram = jnp.dot(picked, picked.T, precision=high, preferred_element_type=jnp.float32)
-    total_gram = lax.psum(partial_gram, ("wide", "narrow"))
+    total_gram = jnp.sum(lax.all_gather(partial_gram, ("wide", "narrow")), axis=0)
     gram = total_gram / jnp.float32(samples.shape[0])
     return (mixed, gram)
 

time: 374 us -> 649 us (1.74)
  blocking collectives: 78.1 us -> 353 us
    all_gather x0 -> x1, blocking collectives: none -> 353 us  [per_device(): lax.all_gather(partial_gram, ('wide', 'narrow'))]
    psum x1 -> x0, blocking collectives: 78.1 us -> none  [per_device(): total_gram = lax.psum(partial_gram, ('wide', 'narrow'))]
  transfers between devices with their start and end apart: 8 -> 8, of which waited for: 7 -> 7; matrix products, arithmetic and copies ran while one was open for 1% -> 0% of each run, Pallas kernels for 0% -> 0%
where the time goes in v1:
time: 649 us
  blocking collectives  353 us (54%)
  waiting for transfers between devices  106 us (16%)
  local copies, waits for them, and re-layouts  104 us (16%)
  other arithmetic  56.5 us (9%)
  matrix products  15.7 us (2%)
  starting transfers between devices  12.8 us (2%)
    all_gather x1, blocking collectives, per_device(): lax.all_gather(partial_gram, ('wide', 'narrow'))  353 us
    ppermute x8, waiting for transfers between devices, partner_2(): return lax.ppermute(value, axis, pairs)  106 us
    gather x1, local copies, waits for them, and re-layouts, per_device(): jnp.take(mixed, clipped, axis=1) * inside.astype(jnp.float32)[None, :]  56.6 us
    select_n x4, other arithmetic, per_device(): jnp.where(narrow_place >> level & 1 == 0, current + partner, partner - cu...  23.4 us
    ppermute x8, local copies, waits for them, and re-layouts, partner_2(): return lax.ppermute(value, axis, pairs)  21 us
    select_n x3, other arithmetic, per_device(): jnp.where(wide_place >> level & 1 == 0, current + partner, partner - curr...  17.6 us
    dot_general x1, matrix products, per_device(): jnp.dot(picked, picked.T, precision=high, preferred_element_type=jnp.floa...  14.3 us
  transfers between devices with their start and end apart: 8, of which 7 were waited for; matrix products, arithmetic and copies ran while one was open for 0% of the time, Pallas kernels for 0%

profile of v1, /device:TPU:1, one launch (start us, length us, event | category | flops | bytes accessed | tf_op | source)
XLA Modules:
  0.0 649.0 jit_solution(8212780732455738130)
XLA Ops:
  0.7 0.8 convert_element_type.6
  1.5 1.1 multiply_bitcast_fusion
  2.7 0.7 fusion.8
  3.4 0.6 fusion.18
  4.1 0.3 copy.38
  4.4 3.3 collective-permute-start
  7.7 2.6 copy.9
  10.3 2.6 copy.10
  13.0 5.9 subtract_select_fusion.6
  18.8 2.8 copy.13
  21.7 13.5 %collective-permute-done.1 = f32[16,8192]{1,0:T(8,128)S(1)} collective-permute-done((f32[16,8192]{1,0:T(8,128)S(1)}, f32[16,8192]{1,0:T(8,128)S(1)}, u32[]{:S(2)}, u32[]{:S(2)}) %collective-permute-start.1) | collective-permute-done | bytes 524320 | tf_op jit(solution)/shard_map/ppermute | solution.py:10
  35.3 2.6 copy.14
  37.9 5.8 subtract_select_fusion.5
  43.7 2.8 copy.16
  46.5 1.3 collective-permute-start.2
  47.8 13.0 %collective-permute-done.2 = f32[16,8192]{1,0:T(8,128)S(1)} collective-permute-done((f32[16,8192]{1,0:T(8,128)S(1)}, f32[16,8192]{1,0:T(8,128)S(1)}, u32[]{:S(2)}, u32[]{:S(2)}) %collective-permute-start.2) | collective-permute-done | bytes 524320 | tf_op jit(solution)/shard_map/ppermute | solution.py:10
  60.7 2.6 copy.17
  63.4 5.9 subtract_select_fusion.4
  69.3 2.8 copy.19
  72.0 1.1 collective-permute-start.3
  73.1 12.2 %collective-permute-done.3 = f32[16,8192]{1,0:T(8,128)S(1)} collective-permute-done((f32[16,8192]{1,0:T(8,128)S(1)}, f32[16,8192]{1,0:T(8,128)S(1)}, u32[]{:S(2)}, u32[]{:S(2)}) %collective-permute-start.3) | collective-permute-done | bytes 524320 | tf_op jit(solution)/shard_map/ppermute | solution.py:10
  85.4 2.6 copy.20
  88.0 5.8 subtract_select_fusion.3
  93.8 2.8 copy.22
  96.7 10.8 %collective-permute-done.4 = f32[16,8192]{1,0:T(8,128)S(1)} collective-permute-done((f32[16,8192]{1,0:T(8,128)S(1)}, f32[16,8192]{1,0:T(8,128)S(1)}, u32[]{:S(2)}, u32[]{:S(2)}) %collective-permute-start.4) | collective-permute-done | bytes 524320 | tf_op jit(solution)/shard_map/ppermute | solution.py:10
  107.5 2.6 copy.23
  110.1 5.9 subtract_select_fusion.2
  116.0 2.8 copy.25
  119.1 9.9 %collective-permute-done.5 = f32[16,8192]{1,0:T(8,128)S(1)} collective-permute-done((f32[16,8192]{1,0:T(8,128)S(1)}, f32[16,8192]{1,0:T(8,128)S(1)}, u32[]{:S(2)}, u32[]{:S(2)}) %collective-permute-start.5) | collective-permute-done | bytes 524320 | tf_op jit(solution)/shard_map/ppermute | solution.py:10
  129.0 2.6 copy.26
  131.6 5.8 subtract_select_fusion.1
  137.4 2.8 copy.28
  140.2 1.7 collective-permute-start.6
  141.9 24.1 %collective-permute-done.6 = f32[16,8192]{1,0:T(8,128)S(1)} collective-permute-done((f32[16,8192]{1,0:T(8,128)S(1)}, f32[16,8192]{1,0:T(8,128)S(1)}, u32[]{:S(2)}, u32[]{:S(2)}) %collective-permute-start.6) | collective-permute-done | bytes 524320 | tf_op jit(solution)/shard_map/ppermute | solution.py:10
  166.0 2.6 copy.29
  168.7 5.9 subtract_select_fusion
  174.5 2.8 copy.31
  177.3 5.0 collective-permute-start.7
  182.4 22.9 %collective-permute-done.7 = f32[16,8192]{1,0:T(8,128)S(1)} collective-permute-done((f32[16,8192]{1,0:T(8,128)S(1)}, f32[16,8192]{1,0:T(8,128)S(1)}, u32[]{:S(2)}, u32[]{:S(2)}) %collective-permute-start.7) | collective-permute-done | bytes 524320 | tf_op jit(solution)/shard_map/ppermute | solution.py:10
  205.4 2.6 copy.32
  208.0 6.0 select_multiply_fusion
  214.0 3.5 copy.34
  217.5 56.6 %gather_fusion = f32[16384,16]{1,0:T(8,128)} fusion(f32[16,8192]{0,1:T(8,128)} %select_multiply_fusion, s32[16384]{0:T(1024)S(1)} %fusion.15), kind=kCustom, calls=%fused_computation | custom fusion | bytes 2162688 | tf_op jit(solution)/shard_map/jit(_take)/gather | solution.py:48
  274.1 6.7 %fusion.78 = f32[16384,16]{1,0:T(8,128)S(1)} fusion(f32[16384,16]{1,0:T(8,128)} %gather_fusion, f32[16384]{0:T(1024)S(1)} %get-tuple-element.7, pred[16384]{0:T(1024)(128)(4,1)S(1)} %get-tuple-element.6), kind=kLoop, calls=%fused_computation.2.clone.2 | loop fusion | flops 524288 | bytes 2179072 | tf_op jit(solution)/shard_map/dot_general | solution.py:49
  280.8 14.3 %fusion = f32[16,16]{1,0:T(8,128)S(1)} fusion(f32[16384,16]{1,0:T(8,128)S(1)} %fusion.78), kind=kOutput, calls=%fused_computation.1 | convolution fusion | flops 50331648 | bytes 1049600 | tf_op jit(solution)/shard_map/dot_general | solution.py:49
  295.1 352.9 %all-gather = f32[4096,16]{1,0:T(8,128)S(1)} all-gather(f32[16,16]{1,0:T(8,128)S(1)} %fusion), channel_id=2, replica_groups=mesh['wide'=16,'narrow'=16] {'wide','narrow'}, dimensions={0}, use_global_device_ids=true | all-gather | bytes 263168 | tf_op jit(solution)/shard_map/all_gather | solution.py:50
  648.1 0.3 reduce_sum.9
  648.4 0.6 broadcast_multiply_fusion
  (16 shorter events, 0.7 us)
Async XLA Ops:
  4.4 5.9 collective-permute-start
  21.6 13.6 %collective-permute-start.1 = (f32[16,8192]{1,0:T(8,128)S(1)}, f32[16,8192]{1,0:T(8,128)S(1)}, u32[]{:S(2)}, u32[]{:S(2)}) collective-permute-start(f32[16,8192]{1,0:T(8,128)S(1)} %copy.13), channel_id=1, source_target_pairs={{0,2},{1,3},{2,0},{3,1},{4,6},{5,7},{6,4},{7,5},{8,10},{9,11},{10,... | collective-permute-start | bytes 1572872 | tf_op jit(solution)/shard_map/ppermute | solution.py:10
  46.5 14.2 %collective-permute-start.2 = (f32[16,8192]{1,0:T(8,128)S(1)}, f32[16,8192]{1,0:T(8,128)S(1)}, u32[]{:S(2)}, u32[]{:S(2)}) collective-permute-start(f32[16,8192]{1,0:T(8,128)S(1)} %copy.16), channel_id=1, source_target_pairs={{0,4},{1,5},{2,6},{3,7},{4,0},{5,1},{6,2},{7,3},{8,12},{9,13},{10,... | collective-permute-start | bytes 1572872 | tf_op jit(solution)/shard_map/ppermute | solution.py:10
  72.0 13.3 %collective-permute-start.3 = (f32[16,8192]{1,0:T(8,128)S(1)}, f32[16,8192]{1,0:T(8,128)S(1)}, u32[]{:S(2)}, u32[]{:S(2)}) collective-permute-start(f32[16,8192]{1,0:T(8,128)S(1)} %copy.19), channel_id=1, source_target_pairs={{0,8},{1,9},{2,10},{3,11},{4,12},{5,13},{6,14},{7,15},{8,0},{9,1},... | collective-permute-start | bytes 1572872 | tf_op jit(solution)/shard_map/ppermute | solution.py:10
  96.6 10.9 %collective-permute-start.4 = (f32[16,8192]{1,0:T(8,128)S(1)}, f32[16,8192]{1,0:T(8,128)S(1)}, u32[]{:S(2)}, u32[]{:S(2)}) collective-permute-start(f32[16,8192]{1,0:T(8,128)S(1)} %copy.22), channel_id=1, source_target_pairs={{0,16},{16,0},{32,48},{48,32},{64,80},{80,64},{96,112},{112,96},{1... | collective-permute-start | bytes 1572872 | tf_op jit(solution)/shard_map/ppermute | solution.py:10
  118.8 10.2 %collective-permute-start.5 = (f32[16,8192]{1,0:T(8,128)S(1)}, f32[16,8192]{1,0:T(8,128)S(1)}, u32[]{:S(2)}, u32[]{:S(2)}) collective-permute-start(f32[16,8192]{1,0:T(8,128)S(1)} %copy.25), channel_id=1, source_target_pairs={{0,32},{16,48},{32,0},{48,16},{64,96},{80,112},{96,64},{112,80},{1... | collective-permute-start | bytes 1572872 | tf_op jit(solution)/shard_map/ppermute | solution.py:10
  140.2 25.8 %collective-permute-start.6 = (f32[16,8192]{1,0:T(8,128)S(1)}, f32[16,8192]{1,0:T(8,128)S(1)}, u32[]{:S(2)}, u32[]{:S(2)}) collective-permute-start(f32[16,8192]{1,0:T(8,128)S(1)} %copy.28), channel_id=1, source_target_pairs={{0,64},{16,80},{32,96},{48,112},{64,0},{80,16},{96,32},{112,48},{1... | collective-permute-start | bytes 1572872 | tf_op jit(solution)/shard_map/ppermute | solution.py:10
  174.5 7.8 %copy-start = (s32[16384]{0:T(1024)S(1)}, s32[16384]{0:T(1024)}, u32[]{:S(2)}) copy-start(s32[16384]{0:T(1024)} %param.5) | copy-start | bytes 196612
  177.3 28.0 %collective-permute-start.7 = (f32[16,8192]{1,0:T(8,128)S(1)}, f32[16,8192]{1,0:T(8,128)S(1)}, u32[]{:S(2)}, u32[]{:S(2)}) collective-permute-start(f32[16,8192]{1,0:T(8,128)S(1)} %copy.31), channel_id=1, source_target_pairs={{0,128},{16,144},{32,160},{48,176},{64,192},{80,208},{96,224},{112... | collective-permute-start | bytes 1572872 | tf_op jit(solution)/shard_map/ppermute | solution.py:10
